TPU v7x, 32 devices: a whole 2x2x4 slice. The times are simulated.
32 devices in a mesh: curve: 4 (over y, x), line: 8 (over z, core).
Axes of the slice: x: 2, y: 2, z: 4, core: 2. Of those that a mesh axis runs over, the one named last changes fastest.
Arguments:
- scaled_distributions: float32 [4, 8, 6, 27, 512], P('curve', 'line'), may hold values from 0.1 to 2.5, as said below
- remaining_brick_places: int32 [4, 8, 6], P('curve', 'line'), may hold values from -1 to 7, as said below
- retained_wavenumbers: int32 [8], replicated, may hold values from 1 to 16, as said below
- regional_amplitudes: float32 [3, 2, 128, 16], P(None, None, 'curve'), may hold values from -0.12 to 0.12
- relaxation_frequencies: float32 [27], replicated, may hold values from 0.6 to 1.8
Outputs:
- new_populations: float32 [4, 8, 6, 27, 512], P('curve', 'line')
Inputs may be any that keep to these rules, and one draw needn't show every extreme that they name: `scaled_distributions`: positive values. `remaining_brick_places`: distinct tile positions (row of the block times 4 plus its column) of one device's surviving blocks, -1 in empty slots, which may stand anywhere; at least half of each device's slots are used, and on some device all 6 are. `retained_wavenumbers`: distinct mode numbers; 16 is always among them.
All inputs are finite; a program needn't handle non-finite values.
Results may differ from a plain program's by a relative error of at most 0.0003.
Values sent between devices are 32-bit elements; how exact they have to be, the bound alone decides.
A program may use at most 64 MiB of HBM per device.

v0:
```python
import jax
import jax.numpy as jnp
import numpy as np
from jax import lax
from jax.sharding import PartitionSpec as P

BE = 16
TX = 4
TY = 2


NUDGE_GAIN = 0.5
TWO_PI = 6.283185307179586
HIGHEST = lax.Precision.HIGHEST


def with_halo(block, sides, width):
    for axis, dim in sides:
        count = lax.axis_size(axis)
        forward = [(i, i + 1) for i in range(count - 1)]
        forward.append((count - 1, 0))
        backward = [(target, source) for source, target in forward]
        low = lax.ppermute(
            lax.slice_in_dim(block, block.shape[dim] - width, None, axis=dim), axis, forward
        )
        high = lax.ppermute(lax.slice_in_dim(block, 0, width, axis=dim), axis, backward)
        block = jnp.concatenate([low, block, high], axis=dim)
    return block


def lattice_tables():
    one_weights = np.array([1.0 / 6.0, 2.0 / 3.0, 1.0 / 6.0])
    speeds = np.array(
        [
            [along_x - 1, along_y - 1, along_z - 1]
            for along_x in range(3)
            for along_y in range(3)
            for along_z in range(3)
        ]
    )
    weights = np.array(
        [
            one_weights[along_x] * one_weights[along_y] * one_weights[along_z]
            for along_x in range(3)
            for along_y in range(3)
            for along_z in range(3)
        ]
    )
    vander = np.array([[1.0, 1.0, 1.0], [-1.0, 0.0, 1.0], [1.0, 0.0, 1.0]])
    undo_vander = np.array([[0.0, -0.5, 0.5], [1.0, 0.0, -1.0], [0.0, 0.5, 0.5]])
    moment_matrix = np.kron(vander, np.kron(vander, vander))
    inverse = np.kron(undo_vander, np.kron(undo_vander, undo_vander))
    forward = jnp.asarray(moment_matrix * weights[None, :], dtype=jnp.float32)
    backward = jnp.asarray(inverse / weights[:, None], dtype=jnp.float32)
    return (forward, backward, speeds)


def mode_basis_at(mode_ids, positions, length):
    phase_ids = positions[:, None] * mode_ids[None, :] % length
    angles = phase_ids.astype(jnp.float32) * (TWO_PI / length)
    return jnp.concatenate([jnp.cos(angles), jnp.sin(angles)], axis=1)


def tile_velocity(moments, safe_density):
    return jnp.stack([moments[9], moments[3], moments[1]], axis=0) / safe_density[None]


def collide_tile(moments, velocity, nudge_tile, backward, relaxation_frequencies):
    density = moments[0]
    shifted = velocity + nudge_tile
    powers = jnp.stack([jnp.ones_like(shifted), shifted, shifted * shifted + 1.0 / 3.0], axis=0)
    equilibrium = (
        density[None, None, None]
        * powers[:, None, None, 0]
        * powers[None, :, None, 1]
        * powers[None, None, :, 2]
    )
    equilibrium = equilibrium.reshape(moments.shape)
    relaxed = moments - relaxation_frequencies[:, None, None, None] * (moments - equilibrium)
    return jnp.einsum("ij,jlrc->ilrc", backward, relaxed, precision=HIGHEST)


def slot_lookup(living_brick_keys, tile_blocks):
    positions = jnp.arange(tile_blocks, dtype=jnp.int32)
    matches = living_brick_keys[None, :] == positions[:, None]
    slot_numbers = jnp.arange(living_brick_keys.shape[0], dtype=jnp.int32)
    slot_of = jnp.sum(jnp.where(matches, slot_numbers[None, :], 0), axis=1)
    present = jnp.any(matches, axis=1)
    return (slot_of, present)


def compact_to_tile(packed_arrangement, slot_of, present, rows_blocks, cols_blocks, block_edge):
    channels = packed_arrangement.shape[1]
    levels = packed_arrangement.shape[2] // (block_edge * block_edge)
    picked = jnp.take(packed_arrangement, slot_of, axis=0) * present[:, None, None].astype(
        packed_arrangement.dtype
    )
    shaped = picked.reshape(rows_blocks, cols_blocks, channels, levels, block_edge, block_edge)
    return shaped.transpose(2, 3, 0, 4, 1, 5).reshape(
        channels, levels, rows_blocks * block_edge, cols_blocks * block_edge
    )


def tile_to_compact(tile_data, living_brick_keys, rows_blocks, cols_blocks, block_edge):
    channels = tile_data.shape[0]
    levels = tile_data.shape[1]
    shaped = tile_data.reshape(
        channels, levels, rows_blocks, block_edge, cols_blocks, block_edge
    ).transpose(2, 4, 0, 1, 3, 5)
    blocks = shaped.reshape(rows_blocks * cols_blocks, channels, levels * block_edge * block_edge)
    occupied_seats = living_brick_keys >= 0
    picked = jnp.take(blocks, jnp.maximum(living_brick_keys, 0), axis=0)
    return picked * occupied_seats[:, None, None].astype(tile_data.dtype)


def on_device(
    scaled_distributions,
    remaining_brick_places,
    retained_wavenumbers,
    regional_amplitudes,
    relaxation_frequencies,
):
    forward, backward, speeds = lattice_tables()
    slot_state = scaled_distributions[0, 0]
    living_brick_keys = remaining_brick_places[0, 0]
    rows_tile = TY * BE
    cols_tile = TX * BE
    slot_of, present = slot_lookup(living_brick_keys, TX * TY)
    fluid_map = present.reshape(TY, TX).astype(jnp.float32)
    fluid_map = jnp.repeat(jnp.repeat(fluid_map, BE, axis=0), BE, axis=1)
    solid_tile = 1.0 - fluid_map
    pops_tile = compact_to_tile(slot_state, slot_of, present, TY, TX, BE)
    moments = jnp.einsum("ij,jlrc->ilrc", forward, pops_tile, precision=HIGHEST)
    safe_density = jnp.where(fluid_map[None] > 0.5, moments[0], 1.0)
    wind_tile = tile_velocity(moments, safe_density)
    line_length = lax.axis_size("line") * cols_tile
    whole_lines = lax.all_to_all(wind_tile, "line", split_axis=2, concat_axis=3, tiled=True)
    rows_each = whole_lines.shape[2]
    mode_basis = mode_basis_at(
        retained_wavenumbers, jnp.arange(line_length, dtype=jnp.int32), line_length
    )
    coefficients = jnp.einsum("klrx,xm->klrm", whole_lines, mode_basis, precision=HIGHEST)
    target = lax.dynamic_slice_in_dim(
        regional_amplitudes, lax.axis_index("line") * rows_each, rows_each, 2
    )
    misfit = target - 2.0 / line_length * coefficients
    forcing_adjustment = NUDGE_GAIN * jnp.einsum(
        "klrm,xm->klrx", misfit, mode_basis, precision=HIGHEST
    )
    nudge_tile = lax.all_to_all(forcing_adjustment, "line", split_axis=3, concat_axis=2, tiled=True)
    post_tile = collide_tile(moments, wind_tile, nudge_tile, backward, relaxation_frequencies)
    levels = post_tile.shape[1]
    solid_plane = jnp.broadcast_to(solid_tile[None, None], (1, levels, rows_tile, cols_tile))
    extended = jnp.concatenate([post_tile, solid_plane], axis=0)
    padded = with_halo(extended, (("curve", 2), ("line", 3)), 1)
    pops_pad = padded[:27]
    solid_pad = padded[27, 0]
    read = []
    for discrete_heading in range(27):
        carry_eastward = int(speeds[discrete_heading, 0])
        carry_northward = int(speeds[discrete_heading, 1])
        step_z = int(speeds[discrete_heading, 2])
        rows_slice = slice(1 - carry_northward, 1 - carry_northward + rows_tile)
        cols_slice = slice(1 - carry_eastward, 1 - carry_eastward + cols_tile)
        carried_sheet = pops_pad[discrete_heading, :, rows_slice, cols_slice]
        blocked = solid_pad[rows_slice, cols_slice] > 0.5
        bounced_distributions = post_tile[26 - discrete_heading]
        if step_z == 0:
            source = carried_sheet
            block_both = jnp.stack([blocked, blocked])
        elif step_z == 1:
            source = jnp.stack([carried_sheet[0], carried_sheet[0]])
            block_both = jnp.stack([jnp.ones_like(blocked), blocked])
        else:
            mirror_sheet = pops_pad[discrete_heading + 2, 1, rows_slice, cols_slice]
            source = jnp.stack([carried_sheet[1], mirror_sheet])
            block_both = jnp.stack([blocked, blocked])
        read.append(jnp.where(block_both, bounced_distributions, source))
    read_tile = jnp.stack(read, axis=0)
    new_state = tile_to_compact(read_tile, living_brick_keys, TY, TX, BE)
    return new_state[None, None]


def solution(mesh):
    return jax.shard_map(
        on_device,
        mesh=mesh,
        in_specs=(
            P("curve", "line", None, None, None),
            P("curve", "line", None),
            P(),
            P(None, None, "curve", None),
            P(),
        ),
        out_specs=P("curve", "line", None, None, None),
        check_vma=False,
    )
```

profile of v0, /device:TPU:0, one launch (start us, length us, event | category | flops | bytes accessed | tf_op | source)
XLA Modules:
  0.0 123.4 jit_solution(8850168669216009851)
XLA Ops:
  0.7 0.8 select_reduce_fusion
  1.4 0.8 fusion.49
  2.3 1.0 copy.391
  4.8 2.9 %gather.13 = f32[2,4,27,2,16,16]{5,4,3,1,0,2:T(8,128)} reshape(f32[8,27,512]{2,0,1:T(8,128)S(1)} %copy.269) | data formatting | bytes 884736 | tf_op jit(solution)/shard_map/jit(_take)/gather | solution.py:95
  7.8 4.6 %multiply_bitcast_fusion = f32[27,2,2,16,4,16]{5,3,1,4,2,0:T(8,128)} fusion(f32[2,4,27,2,16,16]{5,4,3,1,0,2:T(8,128)} %gather.13, f32[2,4]{1,0:T(2,128)S(1)} %reshape.361, pred[2,4]{1,0:T(4,128)(4,1)S(1)} %compare_and_fusion), kind=kLoop, calls=%fused_computation.2 | loop fusion | flops 221184 | bytes 884776 | tf_op jit(solution)/shard_map/transpose | solution.py:99
  12.4 3.6 %copy.270 = f32[27,2,2,16,4,16]{0,5,4,3,2,1:T(8,128)S(1)} copy(f32[27,2,2,16,4,16]{5,3,1,4,2,0:T(8,128)} %multiply_bitcast_fusion) | data formatting | bytes 884736 | tf_op jit(solution)/shard_map/transpose | solution.py:99
  16.4 5.8 %fusion.57 = f32[27,2,32,64]{3,0,2,1:T(8,128)S(1)} fusion(f32[27,27,1,1]{1,0,3,2:T(8,128)S(1)} %copy-done.22, f32[27,2,32,64]{0,3,2,1:T(8,128)S(1)} %bitcast.189), kind=kOutput, calls=%fused_computation.236 | convolution fusion | flops 35831808 | bytes 887652 | tf_op jit(solution)/shard_map/ij,jlrc->ilrc/dot_general | solution.py:133
  23.3 6.3 %all-to-all-start = ((f32[8,1,1536]{2,1,0:T(1,128)}), f32[8,1,1536]{2,1,0:T(1,128)S(1)}, u32[]{:S(2)}, u32[]{:S(2)}) async-start(f32[8,1,1536]{2,1,0:T(1,128)} %reshape.390), calls=%async_computation | async-start | bytes 98304 | tf_op jit(solution)/shard_map/all_to_all | solution.py:137
  29.9 5.5 %all-to-all-done = f32[8,1,1536]{2,1,0:T(1,128)S(1)} async-done(((f32[8,1,1536]{2,1,0:T(1,128)}), f32[8,1,1536]{2,1,0:T(1,128)S(1)}, u32[]{:S(2)}, u32[]{:S(2)}) %all-to-all-start) | async-done | bytes 49184 | tf_op jit(solution)/shard_map/all_to_all | solution.py:137
  37.4 1.1 copy.279
  38.5 3.0 %reshape.392 = f32[8,1,1536]{2,1,0:T(1,128)} reshape(f32[512,3,2,4]{3,2,1,0:T(2,128)S(1)} %bitcast.190) | data formatting | bytes 98304
  41.5 3.7 %all-to-all-start.1 = ((f32[8,1,1536]{2,1,0:T(1,128)}), f32[8,1,1536]{2,1,0:T(1,128)S(1)}, u32[]{:S(2)}, u32[]{:S(2)}) async-start(f32[8,1,1536]{2,1,0:T(1,128)} %reshape.392), calls=%async_computation.1 | async-start | bytes 98304 | tf_op jit(solution)/shard_map/all_to_all | solution.py:150
  45.5 5.2 %all-to-all-done.1 = f32[8,1,1536]{2,1,0:T(1,128)S(1)} async-done(((f32[8,1,1536]{2,1,0:T(1,128)}), f32[8,1,1536]{2,1,0:T(1,128)S(1)}, u32[]{:S(2)}, u32[]{:S(2)}) %all-to-all-start.1) | async-done | bytes 49184 | tf_op jit(solution)/shard_map/all_to_all | solution.py:150
  51.5 2.4 %reshape.393 = f32[512,3,2,4]{3,2,1,0:T(2,128)S(1)} reshape(f32[8,1536]{1,0:T(8,128)S(1)} %reduce.5) | data formatting | bytes 98304
  53.9 1.2 copy.280
  55.5 1.5 %fusion.3 = f32[27,2,32,64]{3,0,2,1:T(8,128)S(1)} fusion(f32[27,27,1,1]{1,0,3,2:T(8,128)S(1)} %copy-done.21, f32[27,2,32,64]{3,0,2,1:T(8,128)S(1)} %fusion.57, f32[27,2,32,64]{3,2,1,0:T(8,128)S(1)} %bitcast.192, f32[27]{0:T(128)S(1)} %copy-done.26), kind=kOutput, calls=%fused_computation.10 | convolution fusion | flops 36163584 | bytes 1330128 | tf_op jit(solution)/shard_map/ij,jlrc->ilrc/dot_general | solution.py:80
  57.6 1.5 %collective-permute-start = (f32[28,2,1,64]{3,2,1,0:T(1,128)S(1)}, f32[28,2,1,64]{3,2,1,0:T(1,128)S(1)}, u32[]{:S(2)}, u32[]{:S(2)}) collective-permute-start(f32[28,2,1,64]{3,2,1,0:T(1,128)S(1)} %get-tuple-element.34), channel_id=1, source_target_pairs={{0,8},{8,16},{16,24},{24,0},{1,9},{9,17},{17,25},{25,1},{2,10},{10... | collective-permute-start | bytes 43016 | tf_op jit(solution)/shard_map/ppermute | solution.py:23
  59.2 1.4 %collective-permute-start.1 = (f32[28,2,1,64]{3,2,1,0:T(1,128)S(1)}, f32[28,2,1,64]{3,2,1,0:T(1,128)S(1)}, u32[]{:S(2)}, u32[]{:S(2)}) collective-permute-start(f32[28,2,1,64]{3,2,1,0:T(1,128)S(1)} %get-tuple-element.35), channel_id=1, source_target_pairs={{8,0},{16,8},{24,16},{0,24},{9,1},{17,9},{25,17},{1,25},{10,2},{18... | collective-permute-start | bytes 43016 | tf_op jit(solution)/shard_map/ppermute | solution.py:26
  61.2 1.6 %collective-permute-done = f32[28,2,1,64]{3,2,1,0:T(1,128)S(1)} collective-permute-done((f32[28,2,1,64]{3,2,1,0:T(1,128)S(1)}, f32[28,2,1,64]{3,2,1,0:T(1,128)S(1)}, u32[]{:S(2)}, u32[]{:S(2)}) %collective-permute-start) | collective-permute-done | bytes 14368 | tf_op jit(solution)/shard_map/ppermute | solution.py:23
  64.6 3.8 %collective-permute-start.3 = (f32[28,2,34,1]{2,1,3,0:T(2,128)S(1)}, f32[28,2,34,1]{2,1,3,0:T(2,128)S(1)}, u32[]{:S(2)}, u32[]{:S(2)}) collective-permute-start(f32[28,2,34,1]{2,1,3,0:T(2,128)S(1)} %copy.286), channel_id=1, source_target_pairs={{1,0},{2,1},{3,2},{4,3},{5,4},{6,5},{7,6},{0,7},{9,8},{10,9},{11,1... | collective-permute-start | bytes 22856 | tf_op jit(solution)/shard_map/ppermute | solution.py:26
  68.4 1.1 fusion.55
  70.2 0.8 stack.344
  73.7 0.8 stack.370
  74.6 0.8 stack.362
  75.4 0.8 stack.361
  76.2 1.4 %fusion.11 = (f32[2,32,64]{2,1,0:T(8,128)}, f32[2,32,64]{2,1,0:T(8,128)}, f32[2,32,64]{2,1,0:T(8,128)}, f32[2,32,64]{2,1,0:T(8,128)S(1)}) fusion(f32[27,2,32,64]{3,2,1,0:T(8,128)S(1)} %copy.284, f32[1,32,64]{2,1,0:T(8,128)} %get-tuple-element.9, pred[1,32,64]{2,1,0:T(8,128)(4,1)S(1)} %bitcast.217, f32[1,32,64]{2,1,0:T(8,128)S(1)} %copy-done.18, ...), kind=kLoop, calls=%fused_computation.67 | loop fusion | flops 32768 | bytes 172032 | tf_op jit(solution)/shard_map/jit(_where)/select_n | solution.py:178
  77.7 0.8 stack.348
  79.2 0.8 fusion.10
  80.0 0.8 stack.343
  80.8 1.4 %maximum_select_fusion.4 = (f32[1,2,32,64]{3,2,1,0:T(8,128)}, f32[1,2,32,64]{3,2,1,0:T(8,128)S(1)}) fusion(f32[28,2,1,64]{3,2,1,0:T(1,128)S(1)} %collective-permute-done.1, f32[1,2,32,64]{3,2,1,0:T(8,128)S(1)} %broadcast_in_dim.80, f32[27,2,32,64]{3,2,1,0:T(8,128)S(1)} %copy.284, pred[1,1,32,64]{3,2,1,0:T(8,128)(4,1)} %bitcast.227), kind=kLoop, calls=%fused_computation.107 | loop fusion | flops 57344 | bytes 1046528 | tf_op jit(solution)/shard_map/jit(_where)/select_n | solution.py:178
  82.1 0.8 stack.334
  83.8 1.5 %maximum_select_fusion.1 = (f32[1,2,32,64]{3,2,1,0:T(8,128)S(1)}, f32[1,2,32,64]{3,2,1,0:T(8,128)}) fusion(f32[28,2,34,1]{3,2,1,0:T(8,128)S(1)} %copy.287, f32[28,2,1,64]{3,2,1,0:T(1,128)S(1)} %collective-permute-done.1, f32[28,2,1,64]{3,2,1,0:T(1,128)S(1)} %collective-permute-done, f32[1,2,32,64]{3,2,1,0:T(8,128)S(1)} %broadcast_in_dim.80, ...), kind=kLoop, calls=%fused_computation.68 | loop fusion | flops 49152 | bytes 3371008 | tf_op jit(solution)/shard_map/jit(_where)/select_n | solution.py:178
  85.2 0.9 stack.317
  86.1 0.8 fusion.29
  87.1 0.9 fusion.21
  88.0 0.8 stack.312
  88.9 0.8 stack.308
  90.5 0.8 stack.321
  91.3 0.8 stack.326
  92.1 0.8 stack.330
  92.9 0.8 stack.335
  95.5 1.6 %copy_dynamic-update-slice_fusion.25 = f32[27,2,2,16,4,16]{5,3,1,4,2,0:T(8,128)} fusion(f32[27,2,2,16,4,16]{5,3,1,4,2,0:T(8,128)} %copy_dynamic-update-slice_fusion.26, f32[1,2,2,16,4,16]{5,4,3,2,1,0:T(4,128)} %stack.308), kind=kLoop, calls=%fused_computation.44 | loop fusion | bytes 262144
  97.1 1.6 %copy_dynamic-update-slice_fusion.24 = f32[27,2,2,16,4,16]{5,3,1,4,2,0:T(8,128)} fusion(f32[27,2,2,16,4,16]{5,3,1,4,2,0:T(8,128)} %copy_dynamic-update-slice_fusion.25, f32[1,2,2,16,4,16]{5,4,3,2,1,0:T(4,128)} %stack.312), kind=kLoop, calls=%fused_computation.43 | loop fusion | bytes 262144
  100.0 1.6 %copy_dynamic-update-slice_fusion.21 = f32[27,2,2,16,4,16]{5,3,1,4,2,0:T(8,128)} fusion(f32[27,2,2,16,4,16]{5,3,1,4,2,0:T(8,128)} %copy_dynamic-update-slice_fusion.22, f32[1,2,2,16,4,16]{5,4,3,2,1,0:T(4,128)} %stack.321), kind=kLoop, calls=%fused_computation.40 | loop fusion | bytes 262144
  102.2 1.6 %copy_dynamic-update-slice_fusion.19 = f32[27,2,2,16,4,16]{5,3,1,4,2,0:T(8,128)} fusion(f32[27,2,2,16,4,16]{5,3,1,4,2,0:T(8,128)} %copy_dynamic-update-slice_fusion.20, f32[1,2,2,16,4,16]{5,4,3,2,1,0:T(4,128)} %stack.326), kind=kLoop, calls=%fused_computation.38 | loop fusion | bytes 262144
  103.7 1.6 %copy_dynamic-update-slice_fusion.18 = f32[27,2,2,16,4,16]{5,3,1,4,2,0:T(8,128)} fusion(f32[27,2,2,16,4,16]{5,3,1,4,2,0:T(8,128)} %copy_dynamic-update-slice_fusion.19, f32[1,2,2,16,4,16]{5,4,3,2,1,0:T(4,128)} %stack.330), kind=kLoop, calls=%fused_computation.37 | loop fusion | bytes 262144
  117.2 4.0 %reshape.360 = f32[8,27,512]{2,0,1:T(8,128)S(1)} reshape(f32[2,4,27,2,16,16]{5,4,3,1,0,2:T(8,128)} %bitcast.193) | data formatting | bytes 884736 | tf_op jit(solution)/shard_map/reshape | solution.py:110
  122.3 1.1 copy.347
  (164 shorter events, 33.2 us)
Async XLA Ops:
  0.0 29.7 %copy-start = (f32[3,2,32,16]{2,3,1,0:T(8,128)S(1)}, f32[3,2,32,16]{2,3,1,0:T(8,128)}, u32[]{:S(2)}) copy-start(f32[3,2,32,16]{2,3,1,0:T(8,128)} %param.10) | copy-start | bytes 36868
  12.4 4.0 %copy-start.22 = (f32[27,27,1,1]{1,0,3,2:T(8,128)S(1)}, f32[27,27,1,1]{1,0,3,2:T(8,128)}, u32[]{:S(2)}) copy-start(f32[27,27,1,1]{1,0,3,2:T(8,128)} %constant.100) | copy-start | bytes 8752
  12.4 17.2 %copy-start.23 = (s32[8]{0:T(128)S(1)}, s32[8]{0:T(128)}, u32[]{:S(2)}) copy-start(s32[8]{0:T(128)} %param.9) | copy-start | bytes 100
  23.3 12.2 %all-to-all-start = ((f32[8,1,1536]{2,1,0:T(1,128)}), f32[8,1,1536]{2,1,0:T(1,128)S(1)}, u32[]{:S(2)}, u32[]{:S(2)}) async-start(f32[8,1,1536]{2,1,0:T(1,128)} %reshape.390), calls=%async_computation | async-start | bytes 98304 | tf_op jit(solution)/shard_map/all_to_all | solution.py:137
  41.5 14.0 %copy-start.21 = (f32[27,27,1,1]{1,0,3,2:T(8,128)S(1)}, f32[27,27,1,1]{1,0,3,2:T(8,128)}, u32[]{:S(2)}) copy-start(f32[27,27,1,1]{1,0,3,2:T(8,128)} %constant.99) | copy-start | bytes 8752
  41.5 14.0 %copy-start.26 = (f32[27]{0:T(128)S(1)}, f32[27]{0:T(128)}, u32[]{:S(2)}) copy-start(f32[27]{0:T(128)} %param.11) | copy-start | bytes 328
  41.5 9.2 %all-to-all-start.1 = ((f32[8,1,1536]{2,1,0:T(1,128)}), f32[8,1,1536]{2,1,0:T(1,128)S(1)}, u32[]{:S(2)}, u32[]{:S(2)}) async-start(f32[8,1,1536]{2,1,0:T(1,128)} %reshape.392), calls=%async_computation.1 | async-start | bytes 98304 | tf_op jit(solution)/shard_map/all_to_all | solution.py:150
  55.3 5.3 %copy-start.27 = (s32[1,1,6]{2,1,0:T(1,128)S(1)}, s32[1,1,6]{2,1,0:T(1,128)}, u32[]{:S(2)}) copy-start(s32[1,1,6]{2,1,0:T(1,128)} %param.8) | copy-start | bytes 76
  57.0 6.0 %copy-start.1 = (f32[27,2,32,64]{3,0,2,1:T(8,128)}, f32[27,2,32,64]{3,0,2,1:T(8,128)S(1)}, u32[]{:S(2)}) copy-start(f32[27,2,32,64]{3,0,2,1:T(8,128)S(1)} %fusion.3) | copy-start | bytes 1327108
  57.6 5.1 %collective-permute-start = (f32[28,2,1,64]{3,2,1,0:T(1,128)S(1)}, f32[28,2,1,64]{3,2,1,0:T(1,128)S(1)}, u32[]{:S(2)}, u32[]{:S(2)}) collective-permute-start(f32[28,2,1,64]{3,2,1,0:T(1,128)S(1)} %get-tuple-element.34), channel_id=1, source_target_pairs={{0,8},{8,16},{16,24},{24,0},{1,9},{9,17},{17,25},{25,1},{2,10},{10... | collective-permute-start | bytes 43016 | tf_op jit(solution)/shard_map/ppermute | solution.py:23
  59.2 3.9 %collective-permute-start.1 = (f32[28,2,1,64]{3,2,1,0:T(1,128)S(1)}, f32[28,2,1,64]{3,2,1,0:T(1,128)S(1)}, u32[]{:S(2)}, u32[]{:S(2)}) collective-permute-start(f32[28,2,1,64]{3,2,1,0:T(1,128)S(1)} %get-tuple-element.35), channel_id=1, source_target_pairs={{8,0},{16,8},{24,16},{0,24},{9,1},{17,9},{25,17},{1,25},{10,2},{18... | collective-permute-start | bytes 43016 | tf_op jit(solution)/shard_map/ppermute | solution.py:26
  64.1 6.9 %collective-permute-start.2 = (f32[28,2,34,1]{2,1,3,0:T(2,128)S(1)}, f32[28,2,34,1]{2,1,3,0:T(2,128)S(1)}, u32[]{:S(2)}, u32[]{:S(2)}) collective-permute-start(f32[28,2,34,1]{2,1,3,0:T(2,128)S(1)} %copy.285), channel_id=1, source_target_pairs={{0,1},{1,2},{2,3},{3,4},{4,5},{5,6},{6,7},{7,0},{8,9},{9,10},{10,1... | collective-permute-start | bytes 22856 | tf_op jit(solution)/shard_map/ppermute | solution.py:23
  64.6 6.8 %collective-permute-start.3 = (f32[28,2,34,1]{2,1,3,0:T(2,128)S(1)}, f32[28,2,34,1]{2,1,3,0:T(2,128)S(1)}, u32[]{:S(2)}, u32[]{:S(2)}) collective-permute-start(f32[28,2,34,1]{2,1,3,0:T(2,128)S(1)} %copy.286), channel_id=1, source_target_pairs={{1,0},{2,1},{3,2},{4,3},{5,4},{6,5},{7,6},{0,7},{9,8},{10,9},{11,1... | collective-permute-start | bytes 22856 | tf_op jit(solution)/shard_map/ppermute | solution.py:26
  72.8 1.8 %copy-start.17 = (pred[32,64]{1,0:T(8,128)(4,1)}, pred[32,64]{1,0:T(8,128)(4,1)S(1)}, u32[]{:S(2)}) copy-start(pred[32,64]{1,0:T(8,128)(4,1)S(1)} %get-tuple-element.50) | copy-start | bytes 6148
  72.8 3.4 %copy-start.16 = (pred[32,64]{1,0:T(8,128)(4,1)}, pred[32,64]{1,0:T(8,128)(4,1)S(1)}, u32[]{:S(2)}) copy-start(pred[32,64]{1,0:T(8,128)(4,1)S(1)} %get-tuple-element.51) | copy-start | bytes 6148
  72.8 3.4 %copy-start.19 = (pred[32,64]{1,0:T(8,128)(4,1)}, pred[32,64]{1,0:T(8,128)(4,1)S(1)}, u32[]{:S(2)}) copy-start(pred[32,64]{1,0:T(8,128)(4,1)S(1)} %get-tuple-element.53) | copy-start | bytes 6148
  73.6 2.6 %copy-start.18 = (f32[1,32,64]{2,1,0:T(8,128)S(1)}, f32[1,32,64]{2,1,0:T(8,128)}, u32[]{:S(2)}) copy-start(f32[1,32,64]{2,1,0:T(8,128)} %get-tuple-element.8) | copy-start | bytes 24580
  87.0 5.9 %copy-start.12 = (f32[1,2,32,64]{3,2,1,0:T(8,128)S(1)}, f32[1,2,32,64]{3,2,1,0:T(8,128)}, u32[]{:S(2)}) copy-start(f32[1,2,32,64]{3,2,1,0:T(8,128)} %get-tuple-element.30) | copy-start | bytes 49156
  87.0 7.5 %copy-start.20 = (pred[32,64]{1,0:T(8,128)(4,1)S(1)}, pred[32,64]{1,0:T(8,128)(4,1)}, u32[]{:S(2)}) copy-start(pred[32,64]{1,0:T(8,128)(4,1)} %copy-done.19) | copy-start | bytes 6148
  88.7 6.0 %copy-start.15 = (f32[2,32,64]{2,1,0:T(8,128)S(1)}, f32[2,32,64]{2,1,0:T(8,128)}, u32[]{:S(2)}) copy-start(f32[2,32,64]{2,1,0:T(8,128)} %get-tuple-element.41) | copy-start | bytes 49156
  88.7 6.1 %copy-start.14 = (f32[2,32,64]{2,1,0:T(8,128)S(1)}, f32[2,32,64]{2,1,0:T(8,128)}, u32[]{:S(2)}) copy-start(f32[2,32,64]{2,1,0:T(8,128)} %get-tuple-element.40) | copy-start | bytes 49156
  88.7 6.4 %copy-start.13 = (f32[2,32,64]{2,1,0:T(8,128)S(1)}, f32[2,32,64]{2,1,0:T(8,128)}, u32[]{:S(2)}) copy-start(f32[2,32,64]{2,1,0:T(8,128)} %get-tuple-element.39) | copy-start | bytes 49156
  89.6 11.9 %copy-start.9 = (f32[1,2,2,16,4,16]{5,4,3,2,1,0:T(4,128)S(1)}, f32[1,2,2,16,4,16]{5,4,3,2,1,0:T(4,128)}, u32[]{:S(2)}) copy-start(f32[1,2,2,16,4,16]{5,4,3,2,1,0:T(4,128)} %stack.325) | copy-start | bytes 49156
  89.6 15.7 %copy-start.8 = (f32[1,2,2,16,4,16]{5,4,3,2,1,0:T(4,128)S(1)}, f32[1,2,2,16,4,16]{5,4,3,2,1,0:T(4,128)}, u32[]{:S(2)}) copy-start(f32[1,2,2,16,4,16]{5,4,3,2,1,0:T(4,128)} %stack.334) | copy-start | bytes 49156
  89.7 17.6 %copy-start.7 = (f32[1,2,2,16,4,16]{5,4,3,2,1,0:T(4,128)S(1)}, f32[1,2,2,16,4,16]{5,4,3,2,1,0:T(4,128)}, u32[]{:S(2)}) copy-start(f32[1,2,2,16,4,16]{5,4,3,2,1,0:T(4,128)} %stack.343) | copy-start | bytes 49156
  89.7 18.2 %copy-start.2 = (f32[1,2,2,16,4,16]{5,4,3,2,1,0:T(4,128)S(1)}, f32[1,2,2,16,4,16]{5,4,3,2,1,0:T(4,128)}, u32[]{:S(2)}) copy-start(f32[1,2,2,16,4,16]{5,4,3,2,1,0:T(4,128)} %stack.344) | copy-start | bytes 49156
  89.8 18.9 %copy-start.6 = (f32[1,2,2,16,4,16]{5,4,3,2,1,0:T(4,128)S(1)}, f32[1,2,2,16,4,16]{5,4,3,2,1,0:T(4,128)}, u32[]{:S(2)}) copy-start(f32[1,2,2,16,4,16]{5,4,3,2,1,0:T(4,128)} %stack.348) | copy-start | bytes 49156
  93.7 17.6 %copy-start.5 = (f32[1,2,2,16,4,16]{5,4,3,2,1,0:T(4,128)S(1)}, f32[1,2,2,16,4,16]{5,4,3,2,1,0:T(4,128)}, u32[]{:S(2)}) copy-start(f32[1,2,2,16,4,16]{5,4,3,2,1,0:T(4,128)} %stack.361) | copy-start | bytes 49156
  94.4 17.5 %copy-start.4 = (f32[1,2,2,16,4,16]{5,4,3,2,1,0:T(4,128)S(1)}, f32[1,2,2,16,4,16]{5,4,3,2,1,0:T(4,128)}, u32[]{:S(2)}) copy-start(f32[1,2,2,16,4,16]{5,4,3,2,1,0:T(4,128)} %stack.362) | copy-start | bytes 49156
  94.5 11.5 %copy-start.10 = (f32[1,2,2,16,4,16]{5,4,3,2,1,0:T(4,128)S(1)}, f32[1,2,2,16,4,16]{5,4,3,2,1,0:T(4,128)}, u32[]{:S(2)}) copy-start(f32[1,2,2,16,4,16]{5,4,3,2,1,0:T(4,128)} %stack.335) | copy-start | bytes 49156
  94.5 12.2 %copy-start.11 = (f32[1,2,2,16,4,16]{5,4,3,2,1,0:T(4,128)S(1)}, f32[1,2,2,16,4,16]{5,4,3,2,1,0:T(4,128)}, u32[]{:S(2)}) copy-start(f32[1,2,2,16,4,16]{5,4,3,2,1,0:T(4,128)} %stack.339) | copy-start | bytes 49156
  94.5 18.8 %copy-start.3 = (f32[1,2,2,16,4,16]{5,4,3,2,1,0:T(4,128)S(1)}, f32[1,2,2,16,4,16]{5,4,3,2,1,0:T(4,128)}, u32[]{:S(2)}) copy-start(f32[1,2,2,16,4,16]{5,4,3,2,1,0:T(4,128)} %stack.370) | copy-start | bytes 49156
  113.9 8.2 %copy-start.24 = (pred[6]{0:T(512)(128)(4,1)S(1)}, pred[6]{0:T(512)(128)(4,1)}, u32[]{:S(2)}) copy-start(pred[6]{0:T(512)(128)(4,1)} %get-tuple-element.59) | copy-start | bytes 22
  113.9 8.2 %copy-start.25 = (f32[6]{0:T(128)S(1)}, f32[6]{0:T(128)}, u32[]{:S(2)}) copy-start(f32[6]{0:T(128)} %get-tuple-element.60) | copy-start | bytes 76
where the time goes:
time: 124 us; the launch traced here: 123 us
  local copies, waits for them, and re-layouts  65.6 us (53%)
  other arithmetic  20.1 us (16%)
  starting transfers between devices  16.8 us (14%)
  waiting for transfers between devices  12.6 us (10%)
  matrix products  7.72 us (6%)
    unnamed x88, local copies, waits for them, and re-layouts  29.1 us
    another operation x28, local copies, waits for them, and re-layouts, on_device(): read_tile = jnp.stack(read, axis=0)  14.4 us
    select_n x14, other arithmetic, on_device(): read.append(jnp.where(block_both, bounced_distributions, source))  7.39 us
    all_to_all x1, starting transfers between devices, on_device(): lax.all_to_all(wind_tile, 'line', split_axis=2, concat_axis=3, tiled=True)  6.32 us
    dot_general x1, matrix products, on_device(): moments = jnp.einsum('ij,jlrc->ilrc', forward, pops_tile, precision=HIGHEST)  5.79 us
    all_to_all x1, waiting for transfers between devices, on_device(): lax.all_to_all(wind_tile, 'line', split_axis=2, concat_axis=3, tiled=True)  5.47 us
    all_to_all x1, waiting for transfers between devices, on_device(): lax.all_to_all(forcing_adjustment, 'line', split_axis=3, concat_axis=2, t...  5.24 us
    ppermute x2, starting transfers between devices, with_halo(): lax.ppermute(lax.slice_in_dim(block, 0, width, axis=dim), axis, backward)  5.22 us
  transfers between devices with their start and end apart: 6, of which 4 were waited for; matrix products, arithmetic and copies ran while one was open for 4% of the time, Pallas kernels for 0%

commit v1 on v0

v1 whole, which is shorter than its diff:
```python
import functools

import jax
import jax.numpy as jnp
import numpy as np
from jax import lax
from jax.experimental import pallas as pl
from jax.experimental.pallas import tpu as pltpu
from jax.sharding import PartitionSpec as P

SLOTS = 6
MESH = pl.DeviceIdType.MESH
TWO_PI = 6.283185307179586
HIGHEST = lax.Precision.HIGHEST


def along(items, stride, fn):
    done = list(items)
    for base in range(27):
        if (base // stride) % 3 == 0:
            at = (base, base + stride, base + 2 * stride)
            got = fn(*(items[n] for n in at))
            for n, value in zip(at, got):
                done[n] = value
    return done


def to_moments(low, mid, high):
    both = (low + high) * (1.0 / 6.0)
    return both + mid * (2.0 / 3.0), (high - low) * (1.0 / 6.0), both


def from_moments(m0, m1, m2):
    return (m2 - m1) * 3.0, (m0 - m2) * 1.5, (m1 + m2) * 3.0


def dot(a, b, dims=((1,), (0,))):
    return lax.dot_general(a, b, (dims, ((), ())), precision=HIGHEST,
                           preferred_element_type=jnp.float32)


def lroll(x, shift):
    shift = shift % 128
    return x if shift == 0 else pltpu.roll(x, shift, 1)


def sroll(x, shift):
    return pltpu.roll(x, shift % 8, 0)


def kernel(nc, nl, keys, waves, rates, x_ref, tgt_ref, out_ref,
           g, post, psend, precv, xsend, xrecv, ysend, yrecv, yside,
           ps_sem, pr_sem, xs_sem, xr_sem, ys_sem, yr_sem, ds_sem, dr_sem):
    ci = lax.axis_index("curve")
    li = lax.axis_index("line")

    def line_at(d):
        return lax.rem(li + (d + nl), nl)

    def curve_at(d):
        return lax.rem(ci + (d + nc), nc)

    barrier = pltpu.get_barrier_semaphore()
    friends = [{"curve": ci, "line": line_at(d)} for d in range(1, nl)]
    friends += [{"curve": curve_at(dy), "line": line_at(dx)} for dy in (-1, 1) for dx in (-1, 0, 1)]
    for friend in friends:
        pl.semaphore_signal(barrier, inc=1, device_id=friend, device_id_type=MESH)

    shape = (8, 128)
    lane = lax.broadcasted_iota(jnp.int32, shape, 1)
    sub = lax.broadcasted_iota(jnp.int32, shape, 0)
    q = lane & 15
    chunk = lane >> 4
    tx = sub & 3
    key = [keys[0, 0, s] for s in range(SLOTS)]

    present = sub == key[0]
    for s in range(1, SLOTS):
        present = jnp.logical_or(present, sub == key[s])
    fluid = jnp.where(present, 1.0, 0.0).astype(jnp.float32)
    solid = 1.0 - fluid

    for p in range(8):
        slot = jnp.int32(0)
        for s in range(SLOTS):
            slot = jnp.where(key[s] == p, s, slot)
        for v in range(4):
            g[v, pl.ds(p, 27, stride=8), :] = x_ref[pl.ds(slot * 108 + v, 27, stride=4), :]

    velocity = [[None] * 4 for _ in range(3)]
    for v in range(4):
        f = [g[v, pl.ds(8 * j, 8), :] for j in range(27)]
        for stride in (1, 3, 9):
            f = along(f, stride, to_moments)
        for j in range(27):
            g[v, pl.ds(8 * j, 8), :] = f[j]
        scale = fluid / f[0]
        for k, j in enumerate((9, 3, 1)):
            velocity[k][v] = f[j] * scale

    def wave_lanes(ids):
        m = ids & 7
        out = jnp.full(ids.shape, waves[0], jnp.int32)
        for n in range(1, 8):
            out = jnp.where(m == n, waves[n], out)
        return out

    total_x = nl * 64
    unit = TWO_PI / total_x
    lane16 = lax.broadcasted_iota(jnp.int32, (16, 128), 1)
    row16 = lax.broadcasted_iota(jnp.int32, (16, 128), 0)
    turn = lax.rem(wave_lanes(lane16) * row16, total_x)
    turn = jnp.where((lane16 & 15) >= 8, turn - total_x // 4, turn)
    small = jnp.cos(turn.astype(jnp.float32) * unit)
    rowb = lax.broadcasted_iota(jnp.int32, (128, 128), 0)
    laneb = lax.broadcasted_iota(jnp.int32, (128, 128), 1)
    basis = jnp.where((rowb >> 4) == (laneb >> 4), jnp.concatenate([small] * 8, axis=0), 0.0)

    start = lax.rem(wave_lanes(lane) * ((li * 4 + tx) * 16), total_x)
    angle = start.astype(jnp.float32) * unit
    cos0 = jnp.cos(angle)
    sin0 = jnp.cos((start - total_x // 4).astype(jnp.float32) * unit)
    is_sin = q >= 8
    sin_signed = jnp.where(is_sin, sin0, -sin0)
    cos96 = jnp.concatenate([cos0] * 12, axis=0)
    sin96 = jnp.concatenate([sin_signed] * 12, axis=0)
    is_sin96 = (lax.broadcasted_iota(jnp.int32, (96, 128), 1) & 15) >= 8

    def swapped(t):
        return jnp.where(is_sin96, pltpu.roll(t, 8, 1), pltpu.roll(t, 120, 1))

    r24 = lax.broadcasted_iota(jnp.int32, (24, 96), 0)
    c96 = lax.broadcasted_iota(jnp.int32, (24, 96), 1)
    same = (r24 >> 2) == (c96 >> 4)
    same = jnp.logical_and(same, ((r24 >> 1) & 1) == ((c96 >> 2) & 1))
    same = jnp.logical_and(same, (r24 & 1) == ((c96 >> 3) & 1))
    gather = jnp.where(same, 1.0, 0.0).astype(jnp.float32)

    stack = jnp.concatenate([velocity[k][v] for k in range(3) for v in range(4)], axis=0)
    local = dot(stack, basis)
    local = local * cos96 + swapped(local) * sin96
    psend[...] = dot(gather, local)

    pl.semaphore_wait(barrier, len(friends))

    copies = []
    for d in range(1, nl):
        copy = pltpu.make_async_remote_copy(
            src_ref=psend, dst_ref=precv.at[d - 1], send_sem=ps_sem.at[d - 1],
            recv_sem=pr_sem.at[d - 1], device_id={"curve": ci, "line": line_at(d)},
            device_id_type=MESH)
        copy.start()
        copies.append(copy)
    ry = lax.broadcasted_iota(jnp.int32, (32, 512), 0)
    ly = lax.broadcasted_iota(jnp.int32, (32, 512), 1)
    spread = dot(tgt_ref[...], jnp.where((ly >> 4) == ry, 1.0, 0.0).astype(jnp.float32))
    rm = lax.broadcasted_iota(jnp.int32, (96, 512), 0)
    lm = lax.broadcasted_iota(jnp.int32, (96, 512), 1)
    spread = jnp.where((rm & 15) == (lm & 15), spread, 0.0)
    target = jnp.zeros((24, 128), jnp.float32)
    for yy in range(4):
        pick = jnp.logical_and((r24 >> 2) == (c96 >> 4), (r24 & 3) == yy)
        target = target + dot(jnp.where(pick, 1.0, 0.0).astype(jnp.float32),
                              spread[:, 128 * yy:128 * yy + 128])

    total = psend[...]
    for d in range(1, nl):
        copies[d - 1].wait_recv()
        total = total + precv[d - 1]
    for copy in copies:
        copy.wait_send()

    misfit = 0.5 * (target - (2.0 / total_x) * total)
    wide = dot(gather, misfit, ((0,), (0,)))
    wide = wide * cos96 - swapped(wide) * sin96
    nudge = dot(wide, basis, ((1,), (1,)))

    for v in range(4):
        m = [g[v, pl.ds(8 * j, 8), :] for j in range(27)]
        powers = []
        for k in range(3):
            at = 8 * (4 * k + v)
            shifted = velocity[k][v] + nudge[at:at + 8, :]
            powers.append((None, shifted, shifted * shifted + 1.0 / 3.0))
        relaxed = []
        for a in range(3):
            along_a = m[0] if a == 0 else m[0] * powers[0][a]
            for b in range(3):
                along_b = along_a if b == 0 else along_a * powers[1][b]
                for c in range(3):
                    eq = along_b if c == 0 else along_b * powers[2][c]
                    j = 9 * a + 3 * b + c
                    relaxed.append(m[j] - rates[j] * (m[j] - eq))
        for stride in (1, 3, 9):
            relaxed = along(relaxed, stride, from_moments)
        for j in range(27):
            post[v, pl.ds(8 * j, 8), :] = relaxed[j]

    def at(j, v):
        return post[v, pl.ds(8 * j, 8), :]

    for n, cx in enumerate((1, -1)):
        for v in range(4):
            pack = solid
            for k in range(9):
                moved = lroll(at(9 * (cx + 1) + k, v), k - 15 if cx == 1 else k)
                pack = jnp.where(q == k, moved, pack)
            xsend[n, v] = pack
    for n, cy in enumerate((1, -1)):
        for cx in (-1, 0, 1):
            pack = solid
            for cz in range(3):
                for z in range(2):
                    c = 2 * cz + z
                    j = 9 * (cx + 1) + 3 * (cy + 1) + cz
                    if cy == 1:
                        moved = lroll(at(j, 2 * z + 1), 16 * c - 112)
                    else:
                        moved = lroll(at(j, 2 * z), 16 * c)
                    pack = jnp.where(chunk == c, moved, pack)
            ysend[n, cx + 1] = pack

    halo = []
    for n, cy in enumerate((1, -1)):
        halo.append(pltpu.make_async_remote_copy(
            src_ref=ysend.at[n], dst_ref=yrecv.at[n], send_sem=ys_sem.at[n],
            recv_sem=yr_sem.at[n], device_id={"curve": curve_at(cy), "line": li},
            device_id_type=MESH))
        for e, cx in enumerate((1, -1)):
            halo.append(pltpu.make_async_remote_copy(
                src_ref=ysend.at[n, cx + 1], dst_ref=yside.at[n, e],
                send_sem=ds_sem.at[n, e], recv_sem=dr_sem.at[n, e],
                device_id={"curve": curve_at(cy), "line": line_at(cx)},
                device_id_type=MESH))
    for n, cx in enumerate((1, -1)):
        halo.append(pltpu.make_async_remote_copy(
            src_ref=xsend.at[n], dst_ref=xrecv.at[n], send_sem=xs_sem.at[n],
            recv_sem=xr_sem.at[n], device_id={"curve": ci, "line": line_at(cx)},
            device_id_type=MESH))
    for copy in halo:
        copy.start()
    for copy in halo:
        copy.wait()

    def beside(own, other, cx):
        if cx == 1:
            return jnp.where(tx == 0, sroll(other, 5), sroll(own, 1))
        return jnp.where(tx == 3, sroll(other, 3), sroll(own, 7))

    def x_edge(cx):
        return q == (0 if cx == 1 else 15)

    rows_in = {}
    for n, cy in enumerate((1, -1)):
        for cx in (-1, 0, 1):
            row = yrecv[n, cx + 1]
            if cx != 0:
                near = beside(row, yside[n, 0 if cx == 1 else 1], cx)
                row = jnp.where(x_edge(cx), lroll(near, -15 * cx), lroll(row, cx))
            rows_in[cx, cy] = sroll(row, 4)
    cols_in = {}
    for n, cx in enumerate((1, -1)):
        for v in range(4):
            cols_in[cx, v] = beside(xsend[n, v], xrecv[n, v], cx)

    def step_x(own, cx, k, v):
        if cx == 0:
            return own
        near = lroll(cols_in[cx, v], -k if cx == 1 else 15 - k)
        return jnp.where(x_edge(cx), near, lroll(own, cx))

    def step_y(a0, a1, cx, cy, c):
        if cy == 0:
            return a0, a1
        r0, r1 = lroll(a0, 16 * cy), lroll(a1, 16 * cy)
        if cy == 1:
            row = lroll(rows_in[cx, cy], -16 * c)
            row = jnp.where(sub < 4, row, sroll(r1, 4))
            return jnp.where(lane < 16, row, r0), jnp.where(lane < 16, r0, r1)
        row = lroll(rows_in[cx, cy], 112 - 16 * c)
        row = jnp.where(sub >= 4, row, sroll(r0, 4))
        return jnp.where(lane >= 112, r1, r0), jnp.where(lane >= 112, row, r1)

    for cx in (-1, 0, 1):
        for cy in (-1, 0, 1):
            base = 9 * (cx + 1) + 3 * (cy + 1)
            if cx == 0 and cy == 0:
                blocked = None
            else:
                wall = step_x(solid, cx, 9, 0)
                walls = step_y(wall, wall, cx, cy, 6)
                blocked = [w > 0.5 for w in walls]

            def moved(cz, z):
                j = base + cz
                k = 3 * (cy + 1) + cz
                a = [step_x(at(j, 2 * z + h), cx, k, 2 * z + h) for h in range(2)]
                return step_y(a[0], a[1], cx, cy, 2 * cz + z)

            def put(cz, z, source):
                j = base + cz
                for h in range(2):
                    value = at(26 - j, 2 * z + h)
                    if source is not None:
                        value = source[h] if blocked is None else jnp.where(blocked[h], value, source[h])
                    g[2 * z + h, pl.ds(8 * j, 8), :] = value

            put(1, 0, moved(1, 0))
            put(1, 1, moved(1, 1))
            put(2, 0, None)
            put(2, 1, moved(2, 0))
            put(0, 0, moved(0, 1))
            put(0, 1, moved(2, 1))

    for s in range(SLOTS):
        place = jnp.maximum(key[s], 0)
        keep = jnp.where(key[s] >= 0, 1.0, 0.0).astype(jnp.float32)
        for v in range(4):
            out_ref[pl.ds(108 * s + v, 27, stride=4), :] = g[v, pl.ds(place, 27, stride=8), :] * keep


def solution(mesh):
    nc, nl = mesh.shape["curve"], mesh.shape["line"]

    def on_device(scaled, places, waves, amplitudes, rates):
        x = scaled.reshape(SLOTS * 108, 128)
        target = amplitudes.transpose(0, 1, 3, 2).reshape(96, 32)
        vmem = pl.BlockSpec(memory_space=pltpu.VMEM)
        smem = pl.BlockSpec(memory_space=pltpu.SMEM)
        f32 = jnp.float32
        dma = pltpu.SemaphoreType.DMA
        out = pl.pallas_call(
            functools.partial(kernel, nc, nl),
            out_shape=jax.ShapeDtypeStruct((SLOTS * 108, 128), f32),
            in_specs=[smem, smem, smem, vmem, vmem],
            out_specs=vmem,
            scratch_shapes=[
                pltpu.VMEM((4, 216, 128), f32),
                pltpu.VMEM((4, 216, 128), f32),
                pltpu.VMEM((24, 128), f32),
                pltpu.VMEM((nl - 1, 24, 128), f32),
                pltpu.VMEM((2, 4, 8, 128), f32),
                pltpu.VMEM((2, 4, 8, 128), f32),
                pltpu.VMEM((2, 3, 8, 128), f32),
                pltpu.VMEM((2, 3, 8, 128), f32),
                pltpu.VMEM((2, 2, 8, 128), f32),
                dma((nl - 1,)), dma((nl - 1,)),
                dma((2,)), dma((2,)), dma((2,)), dma((2,)),
                dma((2, 2)), dma((2, 2)),
            ],
            compiler_params=pltpu.CompilerParams(collective_id=0, has_side_effects=True),
        )(places, waves, rates, x, target)
        return out.reshape(1, 1, SLOTS, 27, 512)

    return jax.shard_map(
        on_device,
        mesh=mesh,
        in_specs=(
            P("curve", "line", None, None, None),
            P("curve", "line", None),
            P(),
            P(None, None, "curve", None),
            P(),
        ),
        out_specs=P("curve", "line", None, None, None),
        check_vma=False,
    )
```

time: 124 us -> 20.2 us (0.16)
  local copies, waits for them, and re-layouts: 65.6 us -> 1.93 us
  other arithmetic: 20.1 us -> 0 us
  Pallas kernels: 0 us -> 18.1 us
  starting transfers between devices: 16.8 us -> 0 us
  waiting for transfers between devices: 12.6 us -> 0 us
  matrix products: 7.72 us -> 0 us
    unnamed x88 -> x1, local copies, waits for them, and re-layouts: 29.1 us -> 1.93 us
    pallas_call x0 -> x1, Pallas kernels: none -> 18.1 us  [on_device(): pl.pallas_call(functools.partial(kernel, nc, nl), out_shape=jax.ShapeDtyp...]
    another operation x29 -> x0, local copies, waits for them, and re-layouts: 14.4 us -> none  [the longest x28 14.4 us: on_device(): read_tile = jnp.stack(read, axis=0)]
    all_to_all x2 -> x0, waiting for transfers between devices: 10.7 us -> none  [the longest x1 5.47 us: on_device(): lax.all_to_all(wind_tile, 'line', split_axis=2, concat_axis=3, tiled=True)]
    all_to_all x2 -> x0, starting transfers between devices: 9.98 us -> none  [the longest x1 6.32 us: on_device(): lax.all_to_all(wind_tile, 'line', split_axis=2, concat_axis=3, tiled=True)]
    dot_general x4 -> x0, matrix products: 7.72 us -> none  [the longest x1 5.79 us: on_device(): moments = jnp.einsum('ij,jlrc->ilrc', forward, pops_tile, precision=HIGHEST)]
    select_n x15 -> x0, other arithmetic: 7.39 us -> none  [the longest x14 7.39 us: on_device(): read.append(jnp.where(block_both, bounced_distributions, source))]
    ppermute x4 -> x0, starting transfers between devices: 6.81 us -> none  [the longest x2 5.22 us: with_halo(): lax.ppermute(lax.slice_in_dim(block, 0, width, axis=dim), axis, backward)]
  transfers between devices with their start and end apart: 6 -> 0, of which waited for: 4 -> 0; matrix products, arithmetic and copies ran while one was open for 4% -> 0% of each run, Pallas kernels for 0% -> 0%
where the time goes in v1:
time: 20.2 us; the launch traced here: 20.1 us
  Pallas kernels  18.1 us (90%)
  local copies, waits for them, and re-layouts  1.93 us (10%)
    pallas_call x1, Pallas kernels, on_device(): pl.pallas_call(functools.partial(kernel, nc, nl), out_shape=jax.ShapeDtyp...  18.1 us
    unnamed x1, local copies, waits for them, and re-layouts  1.93 us

profile of v1, /device:TPU:0, one launch (start us, length us, event | category | flops | bytes accessed | tf_op | source)
XLA Modules:
  0.0 20.1 jit_solution(5076226936616442912)
XLA Ops:
  0.0 18.1 %shard_map.55 = f32[648,128]{1,0:T(8,128)} custom-call(s32[1,1,6]{2,1,0:T(1,128)} %keys.1, s32[8]{0:T(128)} %waves.1, f32[27]{0:T(128)} %rates.1, f32[648,128]{1,0:T(8,128)} %bitcast.6, f32[96,32]{1,0:T(8,128)} %bitcast.7), custom_call_target="tpu_custom_call" | custom-call | tf_op jit(solution)/shard_map/pallas_call | solution.py:332
  18.1 1.9 %copy.9 = f32[1,1,6,27,512]{4,1,3,2,0:T(1,128)} copy(f32[1,1,6,27,512]{4,1,3,2,0:T(1,128)} %bitcast.5) | data formatting | bytes 663552

commit v2 on v1

--- a/solution.py
+++ b/solution.py
@@ -48,8 +48,8 @@
     return pltpu.roll(x, shift % 8, 0)
 
 
-def kernel(nc, nl, keys, waves, rates, x_ref, tgt_ref, out_ref,
-           g, post, psend, precv, xsend, xrecv, ysend, yrecv, yside,
+def collide(nc, nl, keys, waves, rates, x_ref, tgt_ref, post, cols_ref, rows_ref,
+           g, psend, precv, xsend, xrecv, ysend, yrecv, yside,
            ps_sem, pr_sem, xs_sem, xr_sem, ys_sem, yr_sem, ds_sem, dr_sem):
     ci = lax.axis_index("curve")
     li = lax.axis_index("line")
@@ -199,13 +199,7 @@
     def at(j, v):
         return post[v, pl.ds(8 * j, 8), :]
 
-    for n, cx in enumerate((1, -1)):
-        for v in range(4):
-            pack = solid
-            for k in range(9):
-                moved = lroll(at(9 * (cx + 1) + k, v), k - 15 if cx == 1 else k)
-                pack = jnp.where(q == k, moved, pack)
-            xsend[n, v] = pack
+    halo = []
     for n, cy in enumerate((1, -1)):
         for cx in (-1, 0, 1):
             pack = solid
@@ -219,26 +213,30 @@
                         moved = lroll(at(j, 2 * z), 16 * c)
                     pack = jnp.where(chunk == c, moved, pack)
             ysend[n, cx + 1] = pack
-
-    halo = []
-    for n, cy in enumerate((1, -1)):
-        halo.append(pltpu.make_async_remote_copy(
-            src_ref=ysend.at[n], dst_ref=yrecv.at[n], send_sem=ys_sem.at[n],
-            recv_sem=yr_sem.at[n], device_id={"curve": curve_at(cy), "line": li},
-            device_id_type=MESH))
         for e, cx in enumerate((1, -1)):
             halo.append(pltpu.make_async_remote_copy(
                 src_ref=ysend.at[n, cx + 1], dst_ref=yside.at[n, e],
                 send_sem=ds_sem.at[n, e], recv_sem=dr_sem.at[n, e],
                 device_id={"curve": curve_at(cy), "line": line_at(cx)},
                 device_id_type=MESH))
+            halo[-1].start()
+        halo.append(pltpu.make_async_remote_copy(
+            src_ref=ysend.at[n], dst_ref=yrecv.at[n], send_sem=ys_sem.at[n],
+            recv_sem=yr_sem.at[n], device_id={"curve": curve_at(cy), "line": li},
+            device_id_type=MESH))
+        halo[-1].start()
     for n, cx in enumerate((1, -1)):
+        for v in range(4):
+            pack = solid
+            for k in range(9):
+                moved = lroll(at(9 * (cx + 1) + k, v), k - 15 if cx == 1 else k)
+                pack = jnp.where(q == k, moved, pack)
+            xsend[n, v] = pack
         halo.append(pltpu.make_async_remote_copy(
             src_ref=xsend.at[n], dst_ref=xrecv.at[n], send_sem=xs_sem.at[n],
             recv_sem=xr_sem.at[n], device_id={"curve": ci, "line": line_at(cx)},
             device_id_type=MESH))
-    for copy in halo:
-        copy.start()
+        halo[-1].start()
     for copy in halo:
         copy.wait()
 
@@ -250,23 +248,40 @@
     def x_edge(cx):
         return q == (0 if cx == 1 else 15)
 
-    rows_in = {}
     for n, cy in enumerate((1, -1)):
         for cx in (-1, 0, 1):
             row = yrecv[n, cx + 1]
             if cx != 0:
                 near = beside(row, yside[n, 0 if cx == 1 else 1], cx)
                 row = jnp.where(x_edge(cx), lroll(near, -15 * cx), lroll(row, cx))
-            rows_in[cx, cy] = sroll(row, 4)
-    cols_in = {}
+            rows_ref[n, cx + 1] = sroll(row, 4)
     for n, cx in enumerate((1, -1)):
         for v in range(4):
-            cols_in[cx, v] = beside(xsend[n, v], xrecv[n, v], cx)
+            cols_ref[n, v] = beside(xsend[n, v], xrecv[n, v], cx)
+
+
+def stream(keys, post, cols_ref, rows_ref, out_ref, g):
+    shape = (8, 128)
+    lane = lax.broadcasted_iota(jnp.int32, shape, 1)
+    sub = lax.broadcasted_iota(jnp.int32, shape, 0)
+    q = lane & 15
+    key = [keys[0, 0, s] for s in range(SLOTS)]
+
+    present = sub == key[0]
+    for s in range(1, SLOTS):
+        present = jnp.logical_or(present, sub == key[s])
+    solid = jnp.where(present, 0.0, 1.0).astype(jnp.float32)
+
+    def at(j, v):
+        return post[v, pl.ds(8 * j, 8), :]
+
+    def x_edge(cx):
+        return q == (0 if cx == 1 else 15)
 
     def step_x(own, cx, k, v):
         if cx == 0:
             return own
-        near = lroll(cols_in[cx, v], -k if cx == 1 else 15 - k)
+        near = lroll(cols_ref[0 if cx == 1 else 1, v], -k if cx == 1 else 15 - k)
         return jnp.where(x_edge(cx), near, lroll(own, cx))
 
     def step_y(a0, a1, cx, cy, c):
@@ -274,10 +289,10 @@
             return a0, a1
         r0, r1 = lroll(a0, 16 * cy), lroll(a1, 16 * cy)
         if cy == 1:
-            row = lroll(rows_in[cx, cy], -16 * c)
+            row = lroll(rows_ref[0 if cy == 1 else 1, cx + 1], -16 * c)
             row = jnp.where(sub < 4, row, sroll(r1, 4))
             return jnp.where(lane < 16, row, r0), jnp.where(lane < 16, r0, r1)
-        row = lroll(rows_in[cx, cy], 112 - 16 * c)
+        row = lroll(rows_ref[0 if cy == 1 else 1, cx + 1], 112 - 16 * c)
         row = jnp.where(sub >= 4, row, sroll(r0, 4))
         return jnp.where(lane >= 112, r1, r0), jnp.where(lane >= 112, row, r1)
 
@@ -329,13 +344,16 @@
         smem = pl.BlockSpec(memory_space=pltpu.SMEM)
         f32 = jnp.float32
         dma = pltpu.SemaphoreType.DMA
-        out = pl.pallas_call(
-            functools.partial(kernel, nc, nl),
-            out_shape=jax.ShapeDtypeStruct((SLOTS * 108, 128), f32),
+        post, cols, rows = pl.pallas_call(
+            functools.partial(collide, nc, nl),
+            out_shape=[
+                jax.ShapeDtypeStruct((4, 216, 128), f32),
+                jax.ShapeDtypeStruct((2, 4, 8, 128), f32),
+                jax.ShapeDtypeStruct((2, 3, 8, 128), f32),
+            ],
             in_specs=[smem, smem, smem, vmem, vmem],
-            out_specs=vmem,
+            out_specs=[vmem] * 3,
             scratch_shapes=[
-                pltpu.VMEM((4, 216, 128), f32),
                 pltpu.VMEM((4, 216, 128), f32),
                 pltpu.VMEM((24, 128), f32),
                 pltpu.VMEM((nl - 1, 24, 128), f32),
@@ -350,6 +368,13 @@
             ],
             compiler_params=pltpu.CompilerParams(collective_id=0, has_side_effects=True),
         )(places, waves, rates, x, target)
+        out = pl.pallas_call(
+            stream,
+            out_shape=jax.ShapeDtypeStruct((SLOTS * 108, 128), f32),
+            in_specs=[smem, vmem, vmem, vmem],
+            out_specs=vmem,
+            scratch_shapes=[pltpu.VMEM((4, 216, 128), f32)],
+        )(places, post, cols, rows)
         return out.reshape(1, 1, SLOTS, 27, 512)
 
     return jax.shard_map(

time: 20.2 us -> 20.1 us (level)
  local copies, waits for them, and re-layouts: 1.93 us -> 0 us
  Pallas kernels: 18.1 us -> 19.9 us
    unnamed x1 -> x0, local copies, waits for them, and re-layouts: 1.93 us -> none
    pallas_call x1 -> x2, Pallas kernels: 18.1 us -> 19.9 us  [the longest x1 17.2 us: on_device(): pl.pallas_call(functools.partial(collide, nc, nl), out_shape=[jax.ShapeDt...]
where the time goes in v2:
time: 20.1 us; the launch traced here: 20 us
  Pallas kernels  19.9 us (99%)
    pallas_call x1, Pallas kernels, on_device(): pl.pallas_call(functools.partial(collide, nc, nl), out_shape=[jax.ShapeDt...  17.2 us
    pallas_call x1, Pallas kernels, on_device(): pl.pallas_call(stream, out_shape=jax.ShapeDtypeStruct((SLOTS * 108, 128),...  2.77 us

profile of v2, /device:TPU:0, one launch (start us, length us, event | category | flops | bytes accessed | tf_op | source)
XLA Modules:
  0.0 20.0 jit_solution(15590141960012949687)
XLA Ops:
  0.0 17.2 %shard_map.55 = (f32[4,216,128]{2,1,0:T(8,128)}, f32[2,4,8,128]{3,2,1,0:T(8,128)}, f32[2,3,8,128]{3,2,1,0:T(8,128)}) custom-call(s32[1,1,6]{2,1,0:T(1,128)} %keys.3, s32[8]{0:T(128)} %waves.1, f32[27]{0:T(128)} %rates.1, f32[648,128]{1,0:T(8,128)} %bitcast.5, f32[96,32]{1,0:T(8,128)} %bitcast.6), custom_call_target="tpu_custom_call" | custom-call | tf_op jit(solution)/shard_map/pallas_call | solution.py:347
  17.2 2.8 %shard_map.56 = f32[648,128]{1,0:T(8,128)} custom-call(s32[1,1,6]{2,1,0:T(1,128)} %keys.3, f32[4,216,128]{2,1,0:T(8,128)} %get-tuple-element.8.post, f32[2,4,8,128]{3,2,1,0:T(8,128)} %get-tuple-element.9.cols_ref, f32[2,3,8,128]{3,2,1,0:T(8,128)} %get-tuple-element.10.rows_ref), custom_call_target="tpu_custom_call" | custom-call | tf_op jit(solution)/shard_map/pallas_call | solution.py:371

commit v3 on v2

--- a/solution.py
+++ b/solution.py
@@ -48,11 +48,16 @@
     return pltpu.roll(x, shift % 8, 0)
 
 
-def collide(nc, nl, keys, waves, rates, x_ref, tgt_ref, post, cols_ref, rows_ref,
-           g, psend, precv, xsend, xrecv, ysend, yrecv, yside,
-           ps_sem, pr_sem, xs_sem, xr_sem, ys_sem, yr_sem, ds_sem, dr_sem):
+def collide(nc, nl, keys, waves, rates, x_in, tgt_in, post_out, cols_ref, rows_ref,
+            x_ref, tgt_ref, post, g, psend, precv, xsend, xrecv, ysend, yrecv, yside,
+           ps_sem, pr_sem, xs_sem, xr_sem, ys_sem, yr_sem, ds_sem, dr_sem, io_sem):
     ci = lax.axis_index("curve")
     li = lax.axis_index("line")
+
+    fetch = pltpu.make_async_copy(x_in, x_ref, io_sem.at[0])
+    fetch.start()
+    fetch_target = pltpu.make_async_copy(tgt_in, tgt_ref, io_sem.at[1])
+    fetch_target.start()
 
     def line_at(d):
         return lax.rem(li + (d + nl), nl)
@@ -80,6 +85,45 @@
     fluid = jnp.where(present, 1.0, 0.0).astype(jnp.float32)
     solid = 1.0 - fluid
 
+    def wave_lanes(ids):
+        m = ids & 7
+        out = jnp.full(ids.shape, waves[0], jnp.int32)
+        for n in range(1, 8):
+            out = jnp.where(m == n, waves[n], out)
+        return out
+
+    total_x = nl * 64
+    unit = TWO_PI / total_x
+    lane16 = lax.broadcasted_iota(jnp.int32, (16, 128), 1)
+    row16 = lax.broadcasted_iota(jnp.int32, (16, 128), 0)
+    turn = lax.rem(wave_lanes(lane16) * row16, total_x)
+    turn = jnp.where((lane16 & 15) >= 8, turn - total_x // 4, turn)
+    small = jnp.cos(turn.astype(jnp.float32) * unit)
+    rowb = lax.broadcasted_iota(jnp.int32, (128, 128), 0)
+    laneb = lax.broadcasted_iota(jnp.int32, (128, 128), 1)
+    basis = jnp.where((rowb >> 4) == (laneb >> 4), jnp.concatenate([small] * 8, axis=0), 0.0)
+
+    start = lax.rem(wave_lanes(lane) * ((li * 4 + tx) * 16), total_x)
+    angle = start.astype(jnp.float32) * unit
+    cos0 = jnp.cos(angle)
+    sin0 = jnp.cos((start - total_x // 4).astype(jnp.float32) * unit)
+    is_sin = q >= 8
+    sin_signed = jnp.where(is_sin, sin0, -sin0)
+    cos96 = jnp.concatenate([cos0] * 12, axis=0)
+    sin96 = jnp.concatenate([sin_signed] * 12, axis=0)
+    is_sin96 = (lax.broadcasted_iota(jnp.int32, (96, 128), 1) & 15) >= 8
+
+    def swapped(t):
+        return jnp.where(is_sin96, pltpu.roll(t, 8, 1), pltpu.roll(t, 120, 1))
+
+    r24 = lax.broadcasted_iota(jnp.int32, (24, 96), 0)
+    c96 = lax.broadcasted_iota(jnp.int32, (24, 96), 1)
+    same = (r24 >> 2) == (c96 >> 4)
+    same = jnp.logical_and(same, ((r24 >> 1) & 1) == ((c96 >> 2) & 1))
+    same = jnp.logical_and(same, (r24 & 1) == ((c96 >> 3) & 1))
+    gather = jnp.where(same, 1.0, 0.0).astype(jnp.float32)
+
+    fetch.wait()
     for p in range(8):
         slot = jnp.int32(0)
         for s in range(SLOTS):
@@ -98,44 +142,6 @@
         for k, j in enumerate((9, 3, 1)):
             velocity[k][v] = f[j] * scale
 
-    def wave_lanes(ids):
-        m = ids & 7
-        out = jnp.full(ids.shape, waves[0], jnp.int32)
-        for n in range(1, 8):
-            out = jnp.where(m == n, waves[n], out)
-        return out
-
-    total_x = nl * 64
-    unit = TWO_PI / total_x
-    lane16 = lax.broadcasted_iota(jnp.int32, (16, 128), 1)
-    row16 = lax.broadcasted_iota(jnp.int32, (16, 128), 0)
-    turn = lax.rem(wave_lanes(lane16) * row16, total_x)
-    turn = jnp.where((lane16 & 15) >= 8, turn - total_x // 4, turn)
-    small = jnp.cos(turn.astype(jnp.float32) * unit)
-    rowb = lax.broadcasted_iota(jnp.int32, (128, 128), 0)
-    laneb = lax.broadcasted_iota(jnp.int32, (128, 128), 1)
-    basis = jnp.where((rowb >> 4) == (laneb >> 4), jnp.concatenate([small] * 8, axis=0), 0.0)
-
-    start = lax.rem(wave_lanes(lane) * ((li * 4 + tx) * 16), total_x)
-    angle = start.astype(jnp.float32) * unit
-    cos0 = jnp.cos(angle)
-    sin0 = jnp.cos((start - total_x // 4).astype(jnp.float32) * unit)
-    is_sin = q >= 8
-    sin_signed = jnp.where(is_sin, sin0, -sin0)
-    cos96 = jnp.concatenate([cos0] * 12, axis=0)
-    sin96 = jnp.concatenate([sin_signed] * 12, axis=0)
-    is_sin96 = (lax.broadcasted_iota(jnp.int32, (96, 128), 1) & 15) >= 8
-
-    def swapped(t):
-        return jnp.where(is_sin96, pltpu.roll(t, 8, 1), pltpu.roll(t, 120, 1))
-
-    r24 = lax.broadcasted_iota(jnp.int32, (24, 96), 0)
-    c96 = lax.broadcasted_iota(jnp.int32, (24, 96), 1)
-    same = (r24 >> 2) == (c96 >> 4)
-    same = jnp.logical_and(same, ((r24 >> 1) & 1) == ((c96 >> 2) & 1))
-    same = jnp.logical_and(same, (r24 & 1) == ((c96 >> 3) & 1))
-    gather = jnp.where(same, 1.0, 0.0).astype(jnp.float32)
-
     stack = jnp.concatenate([velocity[k][v] for k in range(3) for v in range(4)], axis=0)
     local = dot(stack, basis)
     local = local * cos96 + swapped(local) * sin96
@@ -151,6 +157,7 @@
             device_id_type=MESH)
         copy.start()
         copies.append(copy)
+    fetch_target.wait()
     ry = lax.broadcasted_iota(jnp.int32, (32, 512), 0)
     ly = lax.broadcasted_iota(jnp.int32, (32, 512), 1)
     spread = dot(tgt_ref[...], jnp.where((ly >> 4) == ry, 1.0, 0.0).astype(jnp.float32))
@@ -167,8 +174,6 @@
     for d in range(1, nl):
         copies[d - 1].wait_recv()
         total = total + precv[d - 1]
-    for copy in copies:
-        copy.wait_send()
 
     misfit = 0.5 * (target - (2.0 / total_x) * total)
     wide = dot(gather, misfit, ((0,), (0,)))
@@ -195,6 +200,9 @@
             relaxed = along(relaxed, stride, from_moments)
         for j in range(27):
             post[v, pl.ds(8 * j, 8), :] = relaxed[j]
+
+    store = pltpu.make_async_copy(post, post_out, io_sem.at[2])
+    store.start()
 
     def at(j, v):
         return post[v, pl.ds(8 * j, 8), :]
@@ -238,7 +246,7 @@
             device_id_type=MESH))
         halo[-1].start()
     for copy in halo:
-        copy.wait()
+        copy.wait_recv()
 
     def beside(own, other, cx):
         if cx == 1:
@@ -258,9 +266,12 @@
     for n, cx in enumerate((1, -1)):
         for v in range(4):
             cols_ref[n, v] = beside(xsend[n, v], xrecv[n, v], cx)
-
-
-def stream(keys, post, cols_ref, rows_ref, out_ref, g):
+    for copy in copies + halo:
+        copy.wait_send()
+    store.wait()
+
+
+def stream(keys, post, cols_ref, rows_ref, out, g, out_ref, sem):
     shape = (8, 128)
     lane = lax.broadcasted_iota(jnp.int32, shape, 1)
     sub = lax.broadcasted_iota(jnp.int32, shape, 0)
@@ -327,11 +338,18 @@
             put(0, 0, moved(0, 1))
             put(0, 1, moved(2, 1))
 
+    writes = []
     for s in range(SLOTS):
         place = jnp.maximum(key[s], 0)
         keep = jnp.where(key[s] >= 0, 1.0, 0.0).astype(jnp.float32)
         for v in range(4):
             out_ref[pl.ds(108 * s + v, 27, stride=4), :] = g[v, pl.ds(place, 27, stride=8), :] * keep
+        if s % 2 == 1:
+            part = pl.ds(108 * (s - 1), 216)
+            writes.append(pltpu.make_async_copy(out_ref.at[part], out.at[part], sem.at[s // 2]))
+            writes[-1].start()
+    for copy in writes:
+        copy.wait()
 
 
 def solution(mesh):
@@ -341,6 +359,7 @@
         x = scaled.reshape(SLOTS * 108, 128)
         target = amplitudes.transpose(0, 1, 3, 2).reshape(96, 32)
         vmem = pl.BlockSpec(memory_space=pltpu.VMEM)
+        hbm = pl.BlockSpec(memory_space=pl.ANY)
         smem = pl.BlockSpec(memory_space=pltpu.SMEM)
         f32 = jnp.float32
         dma = pltpu.SemaphoreType.DMA
@@ -351,9 +370,12 @@
                 jax.ShapeDtypeStruct((2, 4, 8, 128), f32),
                 jax.ShapeDtypeStruct((2, 3, 8, 128), f32),
             ],
-            in_specs=[smem, smem, smem, vmem, vmem],
-            out_specs=[vmem] * 3,
+            in_specs=[smem, smem, smem, hbm, hbm],
+            out_specs=[hbm, vmem, vmem],
             scratch_shapes=[
+                pltpu.VMEM((SLOTS * 108, 128), f32),
+                pltpu.VMEM((96, 32), f32),
+                pltpu.VMEM((4, 216, 128), f32),
                 pltpu.VMEM((4, 216, 128), f32),
                 pltpu.VMEM((24, 128), f32),
                 pltpu.VMEM((nl - 1, 24, 128), f32),
@@ -364,7 +386,7 @@
                 pltpu.VMEM((2, 2, 8, 128), f32),
                 dma((nl - 1,)), dma((nl - 1,)),
                 dma((2,)), dma((2,)), dma((2,)), dma((2,)),
-                dma((2, 2)), dma((2, 2)),
+                dma((2, 2)), dma((2, 2)), dma((3,)),
             ],
             compiler_params=pltpu.CompilerParams(collective_id=0, has_side_effects=True),
         )(places, waves, rates, x, target)
@@ -372,8 +394,12 @@
             stream,
             out_shape=jax.ShapeDtypeStruct((SLOTS * 108, 128), f32),
             in_specs=[smem, vmem, vmem, vmem],
-            out_specs=vmem,
-            scratch_shapes=[pltpu.VMEM((4, 216, 128), f32)],
+            out_specs=hbm,
+            scratch_shapes=[
+                pltpu.VMEM((4, 216, 128), f32),
+                pltpu.VMEM((SLOTS * 108, 128), f32),
+                dma((SLOTS // 2,)),
+            ],
         )(places, post, cols, rows)
         return out.reshape(1, 1, SLOTS, 27, 512)
 

time: 20.1 us -> 19.7 us (0.980)
  Pallas kernels: 19.9 us -> 19.5 us
    pallas_call x1, Pallas kernels: 17.2 us -> 16.8 us  [on_device(): pl.pallas_call(functools.partial(collide, nc, nl), out_shape=[jax.ShapeDt...]
where the time goes in v3:
time: 19.7 us; the launch traced here: 19.5 us
  Pallas kernels  19.5 us (99%)
    pallas_call x1, Pallas kernels, on_device(): pl.pallas_call(functools.partial(collide, nc, nl), out_shape=[jax.ShapeDt...  16.8 us
    pallas_call x1, Pallas kernels, on_device(): pl.pallas_call(stream, out_shape=jax.ShapeDtypeStruct((SLOTS * 108, 128),...  2.74 us

profile of v3, /device:TPU:0, one launch (start us, length us, event | category | flops | bytes accessed | tf_op | source)
XLA Modules:
  0.0 19.5 jit_solution(8365706390777776068)
XLA Ops:
  0.0 16.8 %shard_map.55 = (f32[4,216,128]{2,1,0:T(8,128)}, f32[2,4,8,128]{3,2,1,0:T(8,128)}, f32[2,3,8,128]{3,2,1,0:T(8,128)}) custom-call(s32[1,1,6]{2,1,0:T(1,128)} %keys.3, s32[8]{0:T(128)} %waves.1, f32[27]{0:T(128)} %rates.1, f32[648,128]{1,0:T(8,128)} %bitcast.5, f32[96,32]{1,0:T(8,128)} %bitcast.6), custom_call_target="tpu_custom_call" | custom-call | tf_op jit(solution)/shard_map/pallas_call | solution.py:366
  16.8 2.7 %shard_map.56 = f32[648,128]{1,0:T(8,128)} custom-call(s32[1,1,6]{2,1,0:T(1,128)} %keys.3, f32[4,216,128]{2,1,0:T(8,128)} %get-tuple-element.8.post, f32[2,4,8,128]{3,2,1,0:T(8,128)} %get-tuple-element.9.cols_ref, f32[2,3,8,128]{3,2,1,0:T(8,128)} %get-tuple-element.10.rows_ref), custom_call_target="tpu_custom_call" | custom-call | tf_op jit(solution)/shard_map/pallas_call | solution.py:393

commit v4 on v3

--- a/solution.py
+++ b/solution.py
@@ -48,8 +48,8 @@
     return pltpu.roll(x, shift % 8, 0)
 
 
-def collide(nc, nl, keys, waves, rates, x_in, tgt_in, post_out, cols_ref, rows_ref,
-            x_ref, tgt_ref, post, g, psend, precv, xsend, xrecv, ysend, yrecv, yside,
+def collide(nc, nl, keys, waves, rates, x_in, tgt_in, post, cols_ref, rows_ref,
+            x_ref, tgt_ref, g, psend, precv, xsend, xrecv, ysend, yrecv, yside,
            ps_sem, pr_sem, xs_sem, xr_sem, ys_sem, yr_sem, ds_sem, dr_sem, io_sem):
     ci = lax.axis_index("curve")
     li = lax.axis_index("line")
@@ -200,9 +200,6 @@
             relaxed = along(relaxed, stride, from_moments)
         for j in range(27):
             post[v, pl.ds(8 * j, 8), :] = relaxed[j]
-
-    store = pltpu.make_async_copy(post, post_out, io_sem.at[2])
-    store.start()
 
     def at(j, v):
         return post[v, pl.ds(8 * j, 8), :]
@@ -268,7 +265,6 @@
             cols_ref[n, v] = beside(xsend[n, v], xrecv[n, v], cx)
     for copy in copies + halo:
         copy.wait_send()
-    store.wait()
 
 
 def stream(keys, post, cols_ref, rows_ref, out, g, out_ref, sem):
@@ -366,16 +362,15 @@
         post, cols, rows = pl.pallas_call(
             functools.partial(collide, nc, nl),
             out_shape=[
-                jax.ShapeDtypeStruct((4, 216, 128), f32),
-                jax.ShapeDtypeStruct((2, 4, 8, 128), f32),
-                jax.ShapeDtypeStruct((2, 3, 8, 128), f32),
+                pltpu.VMEM((4, 216, 128), f32),
+                pltpu.VMEM((2, 4, 8, 128), f32),
+                pltpu.VMEM((2, 3, 8, 128), f32),
             ],
             in_specs=[smem, smem, smem, hbm, hbm],
-            out_specs=[hbm, vmem, vmem],
+            out_specs=[vmem] * 3,
             scratch_shapes=[
                 pltpu.VMEM((SLOTS * 108, 128), f32),
                 pltpu.VMEM((96, 32), f32),
-                pltpu.VMEM((4, 216, 128), f32),
                 pltpu.VMEM((4, 216, 128), f32),
                 pltpu.VMEM((24, 128), f32),
                 pltpu.VMEM((nl - 1, 24, 128), f32),
@@ -386,10 +381,12 @@
                 pltpu.VMEM((2, 2, 8, 128), f32),
                 dma((nl - 1,)), dma((nl - 1,)),
                 dma((2,)), dma((2,)), dma((2,)), dma((2,)),
-                dma((2, 2)), dma((2, 2)), dma((3,)),
+                dma((2, 2)), dma((2, 2)), dma((2,)),
             ],
             compiler_params=pltpu.CompilerParams(collective_id=0, has_side_effects=True),
         )(places, waves, rates, x, target)
+        post, cols, rows = (
+            pltpu.with_memory_space_constraint(a, pltpu.VMEM) for a in (post, cols, rows))
         out = pl.pallas_call(
             stream,
             out_shape=jax.ShapeDtypeStruct((SLOTS * 108, 128), f32),

time: 19.7 us -> 18.7 us (0.949)
  Pallas kernels: 19.5 us -> 18.5 us
    pallas_call x1, Pallas kernels: 16.8 us -> 16.2 us  [on_device(): pl.pallas_call(functools.partial(collide, nc, nl), out_shape=[pltpu.VMEM(...]
    pallas_call x1, Pallas kernels: 2.74 us -> 2.36 us  [on_device(): pl.pallas_call(stream, out_shape=jax.ShapeDtypeStruct((SLOTS * 108, 128),...]
where the time goes in v4:
time: 18.7 us; the launch traced here: 18.5 us
  Pallas kernels  18.5 us (99%)
    pallas_call x1, Pallas kernels, on_device(): pl.pallas_call(functools.partial(collide, nc, nl), out_shape=[pltpu.VMEM(...  16.2 us
    pallas_call x1, Pallas kernels, on_device(): pl.pallas_call(stream, out_shape=jax.ShapeDtypeStruct((SLOTS * 108, 128),...  2.36 us

profile of v4, /device:TPU:0, one launch (start us, length us, event | category | flops | bytes accessed | tf_op | source)
XLA Modules:
  0.0 18.5 jit_solution(8693869965828477564)
XLA Ops:
  0.0 16.2 %shard_map.55 = (f32[4,216,128]{2,1,0:T(8,128)S(1)}, f32[2,4,8,128]{3,2,1,0:T(8,128)S(1)}, f32[2,3,8,128]{3,2,1,0:T(8,128)S(1)}) custom-call(s32[1,1,6]{2,1,0:T(1,128)} %keys.3, s32[8]{0:T(128)} %waves.1, f32[27]{0:T(128)} %rates.1, f32[648,128]{1,0:T(8,128)} %bitcast.5, f32[96,32]{1,0:T(8,128)} %bitcast.6), custom_call_target="tpu_custom_call" | custom-call | tf_op jit(solution)/shard_map/pallas_call | solution.py:362
  16.2 2.4 %shard_map.56 = f32[648,128]{1,0:T(8,128)} custom-call(s32[1,1,6]{2,1,0:T(1,128)} %keys.3, f32[4,216,128]{2,1,0:T(8,128)S(1)} %get-tuple-element.8.post, f32[2,4,8,128]{3,2,1,0:T(8,128)S(1)} %get-tuple-element.9.cols_ref, f32[2,3,8,128]{3,2,1,0:T(8,128)S(1)} %get-tuple-element.10.rows_ref), custom_call_target="tpu_custom_call" | custom-call | tf_op jit(solution)/shard_map/pallas_call | solution.py:390

commit v5 on v4

--- a/solution.py
+++ b/solution.py
@@ -49,7 +49,7 @@
 
 
 def collide(nc, nl, keys, waves, rates, x_in, tgt_in, post, cols_ref, rows_ref,
-            x_ref, tgt_ref, g, psend, precv, xsend, xrecv, ysend, yrecv, yside,
+            x_ref, tgt_ref, g, psend, precv, xsend, xmsg, xrecv, ysend, yrecv, yside,
            ps_sem, pr_sem, xs_sem, xr_sem, ys_sem, yr_sem, ds_sem, dr_sem, io_sem):
     ci = lax.axis_index("curve")
     li = lax.axis_index("line")
@@ -231,14 +231,17 @@
             device_id_type=MESH))
         halo[-1].start()
     for n, cx in enumerate((1, -1)):
+        merged = jnp.zeros(shape, jnp.float32)
         for v in range(4):
             pack = solid
             for k in range(9):
                 moved = lroll(at(9 * (cx + 1) + k, v), k - 15 if cx == 1 else k)
                 pack = jnp.where(q == k, moved, pack)
             xsend[n, v] = pack
+            merged = jnp.where(tx == v, sroll(pack, v - 3 if cx == 1 else v), merged)
+        xmsg[n] = merged
         halo.append(pltpu.make_async_remote_copy(
-            src_ref=xsend.at[n], dst_ref=xrecv.at[n], send_sem=xs_sem.at[n],
+            src_ref=xmsg.at[n], dst_ref=xrecv.at[n], send_sem=xs_sem.at[n],
             recv_sem=xr_sem.at[n], device_id={"curve": ci, "line": line_at(cx)},
             device_id_type=MESH))
         halo[-1].start()
@@ -262,7 +265,11 @@
             rows_ref[n, cx + 1] = sroll(row, 4)
     for n, cx in enumerate((1, -1)):
         for v in range(4):
-            cols_ref[n, v] = beside(xsend[n, v], xrecv[n, v], cx)
+            own, other = xsend[n, v], xrecv[n]
+            if cx == 1:
+                cols_ref[n, v] = jnp.where(tx == 0, sroll(other, -v), sroll(own, 1))
+            else:
+                cols_ref[n, v] = jnp.where(tx == 3, sroll(other, 3 - v), sroll(own, 7))
     for copy in copies + halo:
         copy.wait_send()
 
@@ -375,7 +382,8 @@
                 pltpu.VMEM((24, 128), f32),
                 pltpu.VMEM((nl - 1, 24, 128), f32),
                 pltpu.VMEM((2, 4, 8, 128), f32),
-                pltpu.VMEM((2, 4, 8, 128), f32),
+                pltpu.VMEM((2, 8, 128), f32),
+                pltpu.VMEM((2, 8, 128), f32),
                 pltpu.VMEM((2, 3, 8, 128), f32),
                 pltpu.VMEM((2, 3, 8, 128), f32),
                 pltpu.VMEM((2, 2, 8, 128), f32),

time: 18.7 us -> 18.7 us (level)
  no operation moved by 1% of the time
where the time goes in v5:
time: 18.7 us; the launch traced here: 18.5 us
  Pallas kernels  18.5 us (99%)
    pallas_call x1, Pallas kernels, on_device(): pl.pallas_call(functools.partial(collide, nc, nl), out_shape=[pltpu.VMEM(...  16.2 us
    pallas_call x1, Pallas kernels, on_device(): pl.pallas_call(stream, out_shape=jax.ShapeDtypeStruct((SLOTS * 108, 128),...  2.36 us

profile of v5, /device:TPU:0, one launch (start us, length us, event | category | flops | bytes accessed | tf_op | source)
XLA Modules:
  0.0 18.5 jit_solution(15575180872935323568)
XLA Ops:
  0.0 16.2 %shard_map.55 = (f32[4,216,128]{2,1,0:T(8,128)S(1)}, f32[2,4,8,128]{3,2,1,0:T(8,128)S(1)}, f32[2,3,8,128]{3,2,1,0:T(8,128)S(1)}) custom-call(s32[1,1,6]{2,1,0:T(1,128)} %keys.3, s32[8]{0:T(128)} %waves.1, f32[27]{0:T(128)} %rates.1, f32[648,128]{1,0:T(8,128)} %bitcast.5, f32[96,32]{1,0:T(8,128)} %bitcast.6), custom_call_target="tpu_custom_call" | custom-call | tf_op jit(solution)/shard_map/pallas_call | solution.py:369
  16.2 2.4 %shard_map.56 = f32[648,128]{1,0:T(8,128)} custom-call(s32[1,1,6]{2,1,0:T(1,128)} %keys.3, f32[4,216,128]{2,1,0:T(8,128)S(1)} %get-tuple-element.8.post, f32[2,4,8,128]{3,2,1,0:T(8,128)S(1)} %get-tuple-element.9.cols_ref, f32[2,3,8,128]{3,2,1,0:T(8,128)S(1)} %get-tuple-element.10.rows_ref), custom_call_target="tpu_custom_call" | custom-call | tf_op jit(solution)/shard_map/pallas_call | solution.py:398

commit v6 on v5

--- a/solution.py
+++ b/solution.py
@@ -11,7 +11,7 @@
 SLOTS = 6
 MESH = pl.DeviceIdType.MESH
 TWO_PI = 6.283185307179586
-HIGHEST = lax.Precision.HIGHEST
+PRODUCT = lax.Precision.HIGH
 
 
 def along(items, stride, fn):
@@ -35,7 +35,7 @@
 
 
 def dot(a, b, dims=((1,), (0,))):
-    return lax.dot_general(a, b, (dims, ((), ())), precision=HIGHEST,
+    return lax.dot_general(a, b, (dims, ((), ())), precision=PRODUCT,
                            preferred_element_type=jnp.float32)
 
 

time: 18.7 us -> 18.6 us (level)
  no operation moved by 1% of the time
where the time goes in v6:
time: 18.6 us; the launch traced here: 18.4 us
  Pallas kernels  18.4 us (99%)
    pallas_call x1, Pallas kernels, on_device(): pl.pallas_call(functools.partial(collide, nc, nl), out_shape=[pltpu.VMEM(...  16 us
    pallas_call x1, Pallas kernels, on_device(): pl.pallas_call(stream, out_shape=jax.ShapeDtypeStruct((SLOTS * 108, 128),...  2.36 us

profile of v6, /device:TPU:0, one launch (start us, length us, event | category | flops | bytes accessed | tf_op | source)
XLA Modules:
  0.0 18.4 jit_solution(1763278771827387185)
XLA Ops:
  0.0 16.0 %shard_map.55 = (f32[4,216,128]{2,1,0:T(8,128)S(1)}, f32[2,4,8,128]{3,2,1,0:T(8,128)S(1)}, f32[2,3,8,128]{3,2,1,0:T(8,128)S(1)}) custom-call(s32[1,1,6]{2,1,0:T(1,128)} %keys.3, s32[8]{0:T(128)} %waves.1, f32[27]{0:T(128)} %rates.1, f32[648,128]{1,0:T(8,128)} %bitcast.5, f32[96,32]{1,0:T(8,128)} %bitcast.6), custom_call_target="tpu_custom_call" | custom-call | tf_op jit(solution)/shard_map/pallas_call | solution.py:369
  16.0 2.4 %shard_map.56 = f32[648,128]{1,0:T(8,128)} custom-call(s32[1,1,6]{2,1,0:T(1,128)} %keys.3, f32[4,216,128]{2,1,0:T(8,128)S(1)} %get-tuple-element.8.post, f32[2,4,8,128]{3,2,1,0:T(8,128)S(1)} %get-tuple-element.9.cols_ref, f32[2,3,8,128]{3,2,1,0:T(8,128)S(1)} %get-tuple-element.10.rows_ref), custom_call_target="tpu_custom_call" | custom-call | tf_op jit(solution)/shard_map/pallas_call | solution.py:398
